TPU v7x, 128 devices: a whole 4x4x4 slice. The times are simulated.
128 devices in a mesh: clip: 4 (over x_hi, core), ctx: 32 (over y, z, x_lo).
Axes of the slice: x: 4 (x_hi: 2, x_lo: 2; x = x_hi * 2 + x_lo), y: 4, z: 4, core: 2. Of those that a mesh axis runs over, the one named last changes fastest.
Arguments:
- queries: bfloat16 [32768, 4096], P(('clip', 'ctx')), parts along dimension 0, may hold values from -128 to 128
- keys: bfloat16 [32768, 4096], P(('clip', 'ctx')), parts along dimension 0, may hold values from -8 to 8
- values: bfloat16 [32768, 4096], P(('clip', 'ctx')), parts along dimension 0, may hold values from -6 to 6
- features: bfloat16 [256, 128, 384], P(('clip', 'ctx')), parts along dimension 0, may hold values from -6 to 6
- feat_grad: bfloat16 [256, 128, 384], P(('clip', 'ctx')), parts along dimension 0, may hold values from -6 to 6
- conv_weight: bfloat16 [3, 384, 384], replicated, may hold values from -0.1875 to 0.1875
- head_weight: bfloat16 [4096, 384], replicated, may hold values from -0.3125 to 0.3125
- pattern: int32 [256, 8], P('clip'), parts along dimension 0, may hold values from 0 to 63, as said below
- live_blocks: int32 [256], P('clip'), parts along dimension 0, may hold values from 1 to 8, as said below
Outputs:
- grad_queries: bfloat16 [32768, 4096], P(('clip', 'ctx')), parts along dimension 0
- grad_keys: bfloat16 [32768, 4096], P(('clip', 'ctx')), parts along dimension 0
- grad_values: bfloat16 [32768, 4096], P(('clip', 'ctx')), parts along dimension 0
- conv_weight_grad: float32 [12, 384, 384], P('clip'), parts along dimension 0
There are 4 independent parts, one for each index of `clip`. A program takes and returns all parts, laid end to end along the dimension named above; an argument that names none is the same for every part. Nothing has to cross between parts.
Inputs may be any that keep to these rules, and one draw needn't show every extreme that they name: `pattern`: row i lists 8 different blocks; its first entry is block i, and the blocks at tile distance 1 to 3 either way, counted cyclically modulo 64, come before others. `live_blocks`: tile 0 has all 8 blocks live.
All inputs are finite; a program needn't handle non-finite values.
Results may differ from a plain program's by a relative error of at most 0.03.
Values may be sent and summed in bfloat16 or wider, within the bound.
No kernel may reach another device: no remote copies, remote signals or barrier semaphores. Data moves between devices by JAX's collectives and lax.ppermute only.
A program may use at most 128 MiB of HBM per device.

v0:
```python
import functools
import math

import jax
import jax.numpy as jnp
from jax import lax
from jax.experimental import pallas as pl
from jax.experimental.pallas import tpu as pltpu
from jax.sharding import PartitionSpec as P

DH = 128
BLK = 128
TOGETHER = 4
PROBS_TOGETHER = 8
GROUP = 8
PACKED = 4
NT = (((1,), (1,)), ((), ()))
TN = (((0,), (0,)), ((), ()))
F32 = jnp.float32
BF16 = jnp.bfloat16
KERNEL_LIMIT = 56 * 1024 * 1024
SMALL_LIMIT = 16 * 1024 * 1024
MEDIUM_LIMIT = 32 * 1024 * 1024
HBM_SPEC = pl.BlockSpec(memory_space=pl.ANY)
VMEM_SPEC = pl.BlockSpec(memory_space=pltpu.VMEM)


def rows_of(tile):
    return tile >> 1, pl.ds(pl.multiple_of((tile & 1) * BLK, BLK), BLK)


def by_count(count, most, body):
    for size in range(1, most + 1):
        pl.when(count == size)(functools.partial(body, size))


def order_by_count(live_blocks):
    tiles = live_blocks.shape[0]
    ids = jnp.arange(tiles, dtype=jnp.int32)
    here, there = live_blocks[:, None], live_blocks[None, :]
    ahead = (there > here) | ((there == here) & (ids[None, :] < ids[:, None]))
    rank = jnp.sum(ahead.astype(jnp.int32), axis=1)
    placed = (rank[None, :] == ids[:, None]).astype(jnp.int32)
    return jnp.sum(placed * ids[None, :], axis=1)


def in_hbm(array):
    return pltpu.with_memory_space_constraint(array, pltpu.HBM)


def columns_of(ref, head):
    return ref.at[:, pl.ds(head * DH, DH)]


def pack_kernel(query_ref, key_ref, value_ref, triple_ref, last_ref, held_ref, in_sems, out_sems):
    rows = query_ref.shape[0]
    arrivals = [
        pltpu.make_async_copy(ref, held_ref.at[place], in_sems.at[place])
        for place, ref in enumerate((query_ref, key_ref, value_ref))
    ]
    for copy in arrivals:
        copy.start()
    departures = []
    for place, arrival in enumerate(arrivals):
        arrival.wait()
        for head in range(triple_ref.shape[0]):
            source = held_ref.at[place, :, pl.ds(head * DH, DH)]
            if place < 2:
                target = triple_ref.at[head, pl.ds(place * rows, rows), :]
            else:
                target = last_ref.at[head]
            departures.append(pltpu.make_async_copy(source, target, out_sems.at[place, head]))
            departures[-1].start()
    for copy in departures:
        copy.wait()


def pack(queries, keys, values, held):
    rows, width = queries.shape
    heads = width // DH
    return pl.pallas_call(
        pack_kernel,
        in_specs=[HBM_SPEC] * 3,
        out_specs=[HBM_SPEC] * 2,
        out_shape=[
            pltpu.HBM((heads, 3 * rows + held, DH), BF16),
            pltpu.HBM((heads, rows, DH), BF16),
        ],
        scratch_shapes=[
            pltpu.VMEM((3, rows, width), BF16),
            pltpu.SemaphoreType.DMA((3,)),
            pltpu.SemaphoreType.DMA((3, heads)),
        ],
        compiler_params=pltpu.CompilerParams(vmem_limit_bytes=SMALL_LIMIT),
        cost_estimate=pl.CostEstimate(flops=0, bytes_accessed=12 * rows * width, transcendentals=0),
    )(in_hbm(queries), in_hbm(keys), in_hbm(values))


def decoder_kernel(
    near_ref,
    next_ref,
    feature_ref,
    tap_weight_ref,
    head_weight_ref,
    triple_in_ref,
    triple_ref,
    held_ref,
    taps_ref,
    grad_sems,
    tap_sems,
):
    heads, rows, _ = held_ref.shape
    frames, positions, channels = feature_ref.shape
    devices = triple_ref.shape[0]
    share = taps_ref.shape[0] // devices
    steps = [near_ref[f] for f in range(frames)] + [next_ref[f] for f in range(frames)]
    taps = tap_weight_ref.shape[0]
    windows = [jnp.concatenate(steps[k : k + frames], 0) for k in range(taps)]
    feature_grad = sum(
        lax.dot_general(windows[k], tap_weight_ref[k], NT, preferred_element_type=F32)
        for k in range(taps)
    ).astype(BF16)
    copies = []
    for first in range(0, heads, PACKED):
        projected = lax.dot_general(
            feature_grad,
            head_weight_ref[first * DH : (first + PACKED) * DH, :],
            NT,
            preferred_element_type=F32,
        ).astype(BF16)
        for head in range(PACKED):
            held_ref[first + head] = projected[:, head * DH : (head + 1) * DH]
        group = pl.ds(first, PACKED)
        copies.append(
            pltpu.make_async_copy(
                held_ref.at[group],
                triple_ref.at[group, pl.ds(2 * rows, rows), :],
                grad_sems.at[first // PACKED],
            )
        )
        copies[-1].start()
    features_t = jnp.concatenate([feature_ref[f] for f in range(frames)], 0).T
    row = 0
    for k in range(taps):
        terms = jnp.dot(features_t, windows[k], preferred_element_type=F32).astype(BF16)
        for first in range(0, channels, DH):
            taps_ref[row : row + channels, :] = terms[:, first : first + DH]
            row += channels
    taps_ref[row:, :] = jnp.zeros((taps_ref.shape[0] - row, DH), BF16)
    for device in range(devices):
        copies.append(
            pltpu.make_async_copy(
                taps_ref.at[pl.ds(device * share, share), :],
                triple_ref.at[device, pl.ds(3 * rows, share), :],
                tap_sems.at[device],
            )
        )
        copies[-1].start()
    for copy in copies:
        copy.wait()


def decoder(feat_grad, incoming, features, conv_weight, head_weight, triple):
    heads, rows = triple.shape[0], features.shape[0] * features.shape[1]
    share = triple.shape[1] - 3 * rows
    return pl.pallas_call(
        decoder_kernel,
        in_specs=[VMEM_SPEC] * 5 + [HBM_SPEC],
        out_specs=HBM_SPEC,
        out_shape=pltpu.HBM(triple.shape, triple.dtype),
        scratch_shapes=[
            pltpu.VMEM((heads, rows, DH), BF16),
            pltpu.VMEM((heads * share, DH), BF16),
            pltpu.SemaphoreType.DMA((heads // PACKED,)),
            pltpu.SemaphoreType.DMA((heads,)),
        ],
        input_output_aliases={5: 0},
        compiler_params=pltpu.CompilerParams(vmem_limit_bytes=MEDIUM_LIMIT),
        cost_estimate=pl.CostEstimate(
            flops=2 * heads * rows * DH * head_weight.shape[1],
            bytes_accessed=6 * heads * rows * DH,
            transcendentals=0,
        ),
    )(feat_grad, incoming, features, conv_weight, head_weight, in_hbm(triple))


def unpack_kernel(factor, pair_ref, last_ref, *refs):
    *out_refs, tap_out_ref, taps_ref, scaled_ref, out_sems, done_sem = refs
    heads, rows = pair_ref.shape[0], out_refs[0].shape[0]
    share = last_ref.shape[1] - rows
    departures = []
    for part, (ref, start) in enumerate([(pair_ref, 0), (pair_ref, rows), (last_ref, 0)]):
        for head in range(heads):
            source = ref.at[head, pl.ds(start, rows), :]
            departures.append(
                pltpu.make_async_copy(
                    source, columns_of(out_refs[part], head), out_sems.at[part, head]
                )
            )
            departures[-1].start()
    for head in range(heads):
        taps_ref[head * share : (head + 1) * share, :] = last_ref[head, rows:, :]
    taps, channels, width = scaled_ref.shape
    row = 0
    for k in range(taps):
        for first in range(0, width, DH):
            terms = taps_ref[row : row + channels, :].astype(F32) * factor
            scaled_ref[k, :, first : first + DH] = terms
            row += channels
    departures.append(pltpu.make_async_copy(scaled_ref, tap_out_ref, done_sem))
    departures[-1].start()
    for copy in departures:
        copy.wait()


def unpack(pair, last, tap_shape, factor):
    heads, rows = pair.shape[0], pair.shape[1] // 2
    return pl.pallas_call(
        functools.partial(unpack_kernel, factor),
        in_specs=[VMEM_SPEC] * 2,
        out_specs=[HBM_SPEC] * 4,
        out_shape=[jax.ShapeDtypeStruct((rows, heads * DH), last.dtype)] * 3
        + [jax.ShapeDtypeStruct(tap_shape, F32)],
        scratch_shapes=[
            pltpu.VMEM((heads * (last.shape[1] - rows), DH), last.dtype),
            pltpu.VMEM(tap_shape, F32),
            pltpu.SemaphoreType.DMA((3, heads)),
            pltpu.SemaphoreType.DMA(()),
        ],
        compiler_params=pltpu.CompilerParams(vmem_limit_bytes=SMALL_LIMIT),
        cost_estimate=pl.CostEstimate(
            flops=0, bytes_accessed=12 * rows * heads * DH, transcendentals=0
        ),
    )(pair, last)


def clear(total_ref):
    def step(block, carry):
        total_ref[block] = jnp.zeros(total_ref.shape[1:], F32)
        return carry

    lax.fori_loop(0, total_ref.shape[0], step, 0)


def gather(ref, blocks, base=0):
    return jnp.concatenate(
        [ref[b >> 1, pl.ds(pl.multiple_of((b & 1) * BLK + base, BLK), BLK), :] for b in blocks], 0
    )


def probs_kernel(
    listed,
    pattern,
    live,
    order,
    query_ref,
    key_ref,
    grad_ref,
    terms_ref,
    probs_ref,
    key_t_ref,
    out_ref,
    total_ref,
    held_ref,
    sem,
):
    scale = DH ** (-0.5) * math.log2(math.e)
    step, steps = pl.program_id(0), pl.num_programs(0)

    rows, held = query_ref.shape[1], held_ref.shape[1]
    arrival = pltpu.make_async_copy(
        terms_ref.at[:, pl.ds(terms_ref.shape[1] - held, held), :], held_ref, sem
    )

    @pl.when(step == 0)
    def _():
        arrival.start()
        clear(total_ref)

    def group_step(group, carry):
        slots = [group * PROBS_TOGETHER + t for t in range(PROBS_TOGETHER)]
        tiles = [order[step * GROUP + slot] for slot in slots]

        def body(size):
            held = []
            for slot, tile in zip(slots, tiles):
                query = query_ref[rows_of(tile)]
                blocks = [pattern[tile * listed + j] for j in range(size)]
                scores = lax.dot_general(
                    gather(key_ref, blocks), query, NT, preferred_element_type=F32
                )
                key_block = lax.broadcasted_iota(jnp.int32, scores.shape, 0) >> 7
                scores = jnp.where(key_block < live[tile], scores, -jnp.inf)
                top = jnp.max(scores, axis=0, keepdims=True)
                weights = jnp.exp2((scores - top) * scale)
                inverse = 1.0 / jnp.sum(weights, axis=0, keepdims=True)
                probs = (weights * inverse).astype(BF16)
                probs_ref[slot, : size * BLK, :] = probs
                terms = jnp.dot(probs, grad_ref[rows_of(tile)], preferred_element_type=F32)
                held.append((blocks, terms))
            for blocks, terms in held:
                for j, b in enumerate(blocks):
                    total_ref[b] += terms[j * BLK : (j + 1) * BLK, :]

        by_count(live[tiles[0]], listed, body)
        for slot in slots:
            key_t_ref[slot] = key_ref[rows_of(step * GROUP + slot)].T
        return carry

    lax.fori_loop(0, GROUP // PROBS_TOGETHER, group_step, 0)

    @pl.when(step == steps - 1)
    def _():
        def finish(block, carry):
            out_ref[rows_of(block)] = total_ref[block].astype(BF16)
            return carry

        lax.fori_loop(0, total_ref.shape[0], finish, 0)
        arrival.wait()
        share = jnp.sum(held_ref[...].astype(F32), axis=0).astype(BF16)
        out_ref[:, rows:, :] = jnp.broadcast_to(share[None], held_ref.shape)


def whole(shape, index=None):
    index = (0,) * len(shape) if index is None else index
    return pl.BlockSpec(shape, lambda i, *_: index, pipeline_mode=pl.Buffered(1))


def probs_of(triple, rows, pattern, live_blocks, order, spare):
    tiles, listed = pattern.shape
    pairs = tiles * listed
    devices = triple.shape[0]
    part = (devices, rows, DH)
    return pl.pallas_call(
        functools.partial(probs_kernel, listed),
        grid_spec=pltpu.PrefetchScalarGridSpec(
            num_scalar_prefetch=3,
            grid=(tiles // GROUP,),
            in_specs=[whole(part, (0, place, 0)) for place in range(3)] + [HBM_SPEC],
            out_specs=[
                pl.BlockSpec((GROUP, listed * BLK, BLK), lambda i, *_: (i, 0, 0)),
                pl.BlockSpec((GROUP, DH, BLK), lambda i, *_: (i, 0, 0)),
                whole((devices, rows + spare, DH)),
            ],
            scratch_shapes=[
                pltpu.VMEM((tiles, BLK, DH), F32),
                pltpu.VMEM((devices, spare, DH), BF16),
                pltpu.SemaphoreType.DMA(()),
            ],
        ),
        out_shape=[
            jax.ShapeDtypeStruct((tiles, listed * BLK, BLK), BF16),
            jax.ShapeDtypeStruct((tiles, DH, BLK), BF16),
            pltpu.HBM((devices, rows + spare, DH), BF16),
        ],
        compiler_params=pltpu.CompilerParams(vmem_limit_bytes=KERNEL_LIMIT),
        cost_estimate=pl.CostEstimate(
            flops=4 * pairs * BLK * BLK * DH,
            bytes_accessed=2 * pairs * BLK * BLK,
            transcendentals=pairs * BLK * BLK,
        ),
    )(pattern.reshape(-1), live_blocks, order, triple, triple, triple, triple)


def grads_kernel(
    listed, pattern, live, order, query_ref, grad_ref, value_ref, key_t_ref, probs_ref, out_ref, total_ref
):
    scale = DH ** (-0.5)
    step, steps = pl.program_id(0), pl.num_programs(0)
    rows = query_ref.shape[1]

    @pl.when(step == 0)
    def _():
        clear(total_ref)

    def group_step(group, carry):
        slots = [group * TOGETHER + t for t in range(TOGETHER)]
        members = [order[step * GROUP + slot] for slot in slots]

        def body(size):
            held = []
            for slot, tile in zip(slots, members):
                blocks = [pattern[tile * listed + j] for j in range(size)]
                dprobs = lax.dot_general(
                    gather(value_ref, blocks), grad_ref[rows_of(tile)], NT, preferred_element_type=F32
                )
                probs = probs_ref[slot, : size * BLK, :].astype(F32)
                delta = jnp.sum(probs * dprobs, axis=0, keepdims=True)
                dscores = (probs * (dprobs - delta)).astype(BF16)
                keys_t = jnp.concatenate([key_t_ref[b] for b in blocks], 1)
                query_grad = jnp.dot(keys_t, dscores, preferred_element_type=F32)
                out_ref[rows_of(tile)] = (query_grad * scale).T.astype(BF16)
                terms = jnp.dot(dscores, query_ref[rows_of(tile)], preferred_element_type=F32)
                held.append((blocks, terms))
            for blocks, terms in held:
                for j, b in enumerate(blocks):
                    total_ref[b] += terms[j * BLK : (j + 1) * BLK, :]

        by_count(live[members[0]], listed, body)
        return carry

    lax.fori_loop(0, GROUP // TOGETHER, group_step, 0)

    @pl.when(step == steps - 1)
    def _():
        def finish(block, carry):
            start = pl.multiple_of((block & 1) * BLK + rows, BLK)
            out_ref[block >> 1, pl.ds(start, BLK), :] = (total_ref[block] * scale).astype(BF16)
            return carry

        lax.fori_loop(0, total_ref.shape[0], finish, 0)


def grads_of(triple, rows, values, keys_t, probs, pattern, live_blocks, order):
    tiles, listed = pattern.shape
    pairs = tiles * listed
    devices = triple.shape[0]
    part = (devices, rows, DH)
    return pl.pallas_call(
        functools.partial(grads_kernel, listed),
        grid_spec=pltpu.PrefetchScalarGridSpec(
            num_scalar_prefetch=3,
            grid=(tiles // GROUP,),
            in_specs=[
                whole(part),
                whole(part, (0, 2, 0)),
                whole(part),
                whole(keys_t.shape),
                pl.BlockSpec((GROUP, listed * BLK, BLK), lambda i, *_: (i, 0, 0)),
            ],
            out_specs=whole((devices, 2 * rows, DH)),
            scratch_shapes=[pltpu.VMEM((tiles, BLK, DH), F32)],
        ),
        out_shape=jax.ShapeDtypeStruct((devices, 2 * rows, DH), BF16),
        compiler_params=pltpu.CompilerParams(vmem_limit_bytes=KERNEL_LIMIT),
        cost_estimate=pl.CostEstimate(
            flops=6 * pairs * BLK * BLK * DH,
            bytes_accessed=2 * pairs * BLK * BLK + 16 * tiles * BLK * DH,
            transcendentals=0,
        ),
    )(pattern.reshape(-1), live_blocks, order, triple, triple, values, keys_t, probs)


def exchange(blocks):
    return lax.all_to_all(blocks, "ctx", split_axis=0, concat_axis=0, tiled=True)


def body(
    queries, keys, values, features, feat_grad, conv_weight, head_weight, pattern, live_blocks
):
    devices = lax.axis_size("ctx")
    frames, positions, channels = features.shape
    rows = frames * positions
    share = -(-conv_weight.size // devices // DH // 16) * 16

    incoming = lax.ppermute(feat_grad, "ctx", [(i + 1, i) for i in range(devices - 1)])
    triple, values = pack(queries, keys, values, share)
    triple, values, incoming = lax.optimization_barrier((triple, values, incoming))
    triple = decoder(feat_grad, incoming, features, conv_weight, head_weight, triple)

    triple = exchange(triple)
    values, triple, pattern, live_blocks = lax.optimization_barrier(
        (values, triple, pattern, live_blocks)
    )
    values = exchange(values)
    order = order_by_count(live_blocks)
    probs, keys_t, value_grad = probs_of(triple, rows, pattern, live_blocks, order, share)

    value_grad, values = lax.optimization_barrier((value_grad, values))
    value_grad = exchange(value_grad)
    grads = grads_of(triple, rows, values, keys_t, probs, pattern, live_blocks, order)
    grads, value_grad = lax.optimization_barrier((grads, value_grad))
    grads = exchange(grads)

    factor = 1.0 / math.sqrt(rows * devices)
    return tuple(unpack(grads, value_grad, conv_weight.shape, factor))


def solution(mesh):
    placed = (
        P(("clip", "ctx"), None),
        P(("clip", "ctx"), None),
        P(("clip", "ctx"), None),
        P(("clip", "ctx"), None, None),
        P(("clip", "ctx"), None, None),
        P(),
        P(),
        P("clip", None),
        P("clip"),
    )
    return jax.shard_map(
        body,
        mesh=mesh,
        in_specs=placed,
        out_specs=(
            P(("clip", "ctx"), None),
            P(("clip", "ctx"), None),
            P(("clip", "ctx"), None),
            P("clip", None, None),
        ),
        check_vma=False,
    )
```

profile of v0, /device:TPU:0, one launch (start us, length us, event | category | flops | bytes accessed | tf_op | source)
XLA Modules:
  0.0 253.3 jit_solution(7020507896651889686)
XLA Ops:
  0.6 0.0 copy-start.2
  0.6 0.0 copy-start
  0.7 0.0 copy-start.1
  0.7 0.0 copy-start.3
  0.7 1.6 collective-permute-start
  2.2 5.6 %shard_map.120 = (bf16[32,880,128]{2,1,0:T(8,128)(2,1)}, bf16[32,256,128]{2,1,0:T(8,128)(2,1)}) custom-call(bf16[256,4096]{1,0:T(8,128)(2,1)} %query_ref.1, bf16[256,4096]{1,0:T(8,128)(2,1)} %key_ref.1, bf16[256,4096]{1,0:T(8,128)(2,1)} %value_ref.1), custom_call_target="tpu_custom_call" | custom-call | bytes 12582912 | tf_op jit(solution)/shard_map/pallas_call | solution.py:81
  7.9 1.7 collective-permute-done.next_ref
  9.5 0.0 copy-done.2
  9.5 0.0 copy-done
  9.5 0.0 copy-done.1
  9.5 0.0 copy-done.3
  9.5 3.5 %shard_map.121 = bf16[32,880,128]{2,1,0:T(8,128)(2,1)} custom-call(bf16[2,128,384]{2,1,0:T(8,128)(2,1)S(1)} %copy-done.2, bf16[2,128,384]{2,1,0:T(8,128)(2,1)S(1)} %collective-permute-done.next_ref, bf16[2,128,384]{2,1,0:T(8,128)(2,1)S(1)} %copy-done.3, bf16[3,384,384]{2,1,0:T(8,128)(2,1)S(1)} %copy-done.1, ...), custom_call_target="tpu_custom_call", output_to_operand_aliasing={{}: (5, {})} | custom-call | flops 805306368 | bytes 6291456 | tf_op jit(solution)/shard_map/pallas_call | solution.py:166
  13.0 95.9 %all_to_all.20.query_ref.key_ref.grad_ref.terms_ref = bf16[32,880,128]{2,1,0:T(8,128)(2,1)} all-to-all(bf16[32,880,128]{2,1,0:T(8,128)(2,1)} %shard_map.121), channel_id=1, replica_groups=mesh['clip'=4,'ctx'=32] {'ctx'}, dimensions={0} | all-to-all | bytes 14417920 | tf_op jit(solution)/shard_map/all_to_all | solution.py:445
  108.9 0.0 copy-start.5
  108.9 0.0 copy-start.6
  108.9 4.1 %all-to-all-start.1 = ((bf16[32,256,128]{2,1,0:T(8,128)(2,1)}), bf16[32,256,128]{2,1,0:T(8,128)(2,1)S(1)}, u32[]{:S(2)}, u32[]{:S(2)}) async-start(bf16[32,256,128]{2,1,0:T(8,128)(2,1)} %get-tuple-element.29), calls=%async_computation.1 | async-start | bytes 4194304 | tf_op jit(solution)/shard_map/all_to_all | solution.py:445
  113.1 0.0 copy-done.5
  113.1 0.1 copy.15
  113.2 0.7 reshape.15.pattern
  113.8 0.0 copy-done.6
  113.8 0.2 convert_reduce_fusion
  114.0 0.6 select_reduce_fusion.order
  114.6 24.1 %shard_map.122 = (bf16[64,1024,128]{2,1,0:T(8,128)(2,1)}, bf16[64,128,128]{2,1,0:T(8,128)(2,1)}, bf16[32,368,128]{2,1,0:T(8,128)(2,1)}) custom-call(s32[512]{0:T(512)} %reshape.15.pattern, s32[64]{0:T(128)} %live.1, s32[64]{0:T(128)} %select_reduce_fusion.order, bf16[32,880,128]{2,1,0:T(8,128)(2,1)} %all_to_all.20.query_ref.key_ref.grad_ref.terms_ref, ...), custom_call_target="tpu_custom_call" | custom-call | flops 4294967296 | bytes 16777216 | tf_op jit(solution)/shard_map/pallas_call | solution.py:334
  138.7 6.4 %all-to-all-done.1.value_ref = bf16[32,256,128]{2,1,0:T(8,128)(2,1)S(1)} async-done(((bf16[32,256,128]{2,1,0:T(8,128)(2,1)}), bf16[32,256,128]{2,1,0:T(8,128)(2,1)S(1)}, u32[]{:S(2)}, u32[]{:S(2)}) %all-to-all-start.1) | async-done | bytes 2097184 | tf_op jit(solution)/shard_map/all_to_all | solution.py:445
  145.1 0.0 copy-start.4
  145.1 1.3 copy-done.4
  146.4 4.3 %all-to-all-start.2 = ((bf16[32,368,128]{2,1,0:T(8,128)(2,1)}), bf16[32,368,128]{2,1,0:T(8,128)(2,1)S(1)}, u32[]{:S(2)}, u32[]{:S(2)}) async-start(bf16[32,368,128]{2,1,0:T(8,128)(2,1)} %get-tuple-element.33), calls=%async_computation.2 | async-start | bytes 6029312 | tf_op jit(solution)/shard_map/all_to_all | solution.py:445
  150.7 34.1 %shard_map.123 = bf16[32,512,128]{2,1,0:T(8,128)(2,1)} custom-call(s32[512]{0:T(512)} %reshape.15.pattern, s32[64]{0:T(128)} %live.1, s32[64]{0:T(128)} %select_reduce_fusion.order, bf16[32,880,128]{2,1,0:T(8,128)(2,1)} %all_to_all.20.query_ref.key_ref.grad_ref.terms_ref, bf16[32,880,128]{2,1,0:T(8,128)(2,1)} %all_to_all.20.query_ref.key_ref.grad_ref.terms_ref, ...), custom_call_target="tpu_custom_call" | custom-call | flops 6442450944 | bytes 33554432 | tf_op jit(solution)/shard_map/pallas_call | solution.py:419
  184.8 9.3 %all-to-all-done.2.last_ref = bf16[32,368,128]{2,1,0:T(8,128)(2,1)S(1)} async-done(((bf16[32,368,128]{2,1,0:T(8,128)(2,1)}), bf16[32,368,128]{2,1,0:T(8,128)(2,1)S(1)}, u32[]{:S(2)}, u32[]{:S(2)}) %all-to-all-start.2) | async-done | bytes 3014688 | tf_op jit(solution)/shard_map/all_to_all | solution.py:445
  194.1 55.0 %all_to_all.21.pair_ref = bf16[32,512,128]{2,1,0:T(8,128)(2,1)S(1)} all-to-all(bf16[32,512,128]{2,1,0:T(8,128)(2,1)} %shard_map.123), channel_id=1, replica_groups=mesh['clip'=4,'ctx'=32] {'ctx'}, dimensions={0} | all-to-all | bytes 8388608 | tf_op jit(solution)/shard_map/all_to_all | solution.py:445
  249.1 4.0 %shard_map.124 = (bf16[256,4096]{1,0:T(8,128)(2,1)}, bf16[256,4096]{1,0:T(8,128)(2,1)}, bf16[256,4096]{1,0:T(8,128)(2,1)}, f32[3,384,384]{2,1,0:T(8,128)}) custom-call(bf16[32,512,128]{2,1,0:T(8,128)(2,1)S(1)} %all_to_all.21.pair_ref, bf16[32,368,128]{2,1,0:T(8,128)(2,1)S(1)} %all-to-all-done.2.last_ref), custom_call_target="tpu_custom_call" | custom-call | bytes 12582912 | tf_op jit(solution)/shard_map/pallas_call | solution.py:218
Async XLA Ops:
  0.6 8.9 %copy-start.2 = (bf16[2,128,384]{2,1,0:T(8,128)(2,1)S(1)}, bf16[2,128,384]{2,1,0:T(8,128)(2,1)}, u32[]{:S(2)}) copy-start(bf16[2,128,384]{2,1,0:T(8,128)(2,1)} %near_ref.1) | copy-start | bytes 589828
  0.6 8.9 %copy-start = (bf16[4096,384]{1,0:T(8,128)(2,1)S(1)}, bf16[4096,384]{1,0:T(8,128)(2,1)}, u32[]{:S(2)}) copy-start(bf16[4096,384]{1,0:T(8,128)(2,1)} %head_weight_ref.1) | copy-start | bytes 9437188
  0.7 8.9 %copy-start.1 = (bf16[3,384,384]{2,1,0:T(8,128)(2,1)S(1)}, bf16[3,384,384]{2,1,0:T(8,128)(2,1)}, u32[]{:S(2)}) copy-start(bf16[3,384,384]{2,1,0:T(8,128)(2,1)} %tap_weight_ref.1) | copy-start | bytes 2654212
  0.7 8.9 %copy-start.3 = (bf16[2,128,384]{2,1,0:T(8,128)(2,1)S(1)}, bf16[2,128,384]{2,1,0:T(8,128)(2,1)}, u32[]{:S(2)}) copy-start(bf16[2,128,384]{2,1,0:T(8,128)(2,1)} %feature_ref.1) | copy-start | bytes 589828
  0.7 8.8 %collective-permute-start = (bf16[2,128,384]{2,1,0:T(8,128)(2,1)}, bf16[2,128,384]{2,1,0:T(8,128)(2,1)S(1)}, u32[]{:S(2)}, u32[]{:S(2)}) collective-permute-start(bf16[2,128,384]{2,1,0:T(8,128)(2,1)} %near_ref.1), channel_id=1, source_target_pairs={{1,0},{2,1},{3,2},{4,3},{5,4},{6,5},{7,6},{8,7},{9,8},{10,9},{11,1... | collective-permute-start | bytes 589832 | tf_op jit(solution)/shard_map/ppermute | solution.py:456
  108.9 4.2 %copy-start.5 = (s32[64,8]{0,1:T(8,128)S(1)}, s32[64,8]{0,1:T(8,128)}, u32[]{:S(2)}) copy-start(s32[64,8]{0,1:T(8,128)} %param.16) | copy-start | bytes 6148
  108.9 4.9 %copy-start.6 = (s32[64]{0:T(128)S(1)}, s32[64]{0:T(128)}, u32[]{:S(2)}) copy-start(s32[64]{0:T(128)} %live.1) | copy-start | bytes 772
  108.9 36.2 %all-to-all-start.1 = ((bf16[32,256,128]{2,1,0:T(8,128)(2,1)}), bf16[32,256,128]{2,1,0:T(8,128)(2,1)S(1)}, u32[]{:S(2)}, u32[]{:S(2)}) async-start(bf16[32,256,128]{2,1,0:T(8,128)(2,1)} %get-tuple-element.29), calls=%async_computation.1 | async-start | bytes 4194304 | tf_op jit(solution)/shard_map/all_to_all | solution.py:445
  145.1 1.3 copy-start.4
  146.4 47.7 %all-to-all-start.2 = ((bf16[32,368,128]{2,1,0:T(8,128)(2,1)}), bf16[32,368,128]{2,1,0:T(8,128)(2,1)S(1)}, u32[]{:S(2)}, u32[]{:S(2)}) async-start(bf16[32,368,128]{2,1,0:T(8,128)(2,1)} %get-tuple-element.33), calls=%async_computation.2 | async-start | bytes 6029312 | tf_op jit(solution)/shard_map/all_to_all | solution.py:445
where the time goes:
time: 254 us; the launch traced here: 253 us
  blocking collectives  151 us (59%)
  Pallas kernels  71.3 us (28%)
  waiting for transfers between devices  17.4 us (7%)
  starting transfers between devices  9.98 us (4%)
    all_to_all x2, blocking collectives, exchange(): lax.all_to_all(blocks, 'ctx', split_axis=0, concat_axis=0, tiled=True)  151 us
    pallas_call x1, Pallas kernels, grads_of(): pl.pallas_call(functools.partial(grads_kernel, listed), grid_spec=pltpu.P...  34.1 us
    pallas_call x1, Pallas kernels, probs_of(): pl.pallas_call(functools.partial(probs_kernel, listed), grid_spec=pltpu.P...  24.1 us
    all_to_all x2, waiting for transfers between devices, exchange(): lax.all_to_all(blocks, 'ctx', split_axis=0, concat_axis=0, tiled=True)  15.7 us
    all_to_all x2, starting transfers between devices, exchange(): lax.all_to_all(blocks, 'ctx', split_axis=0, concat_axis=0, tiled=True)  8.43 us
    pallas_call x1, Pallas kernels, pack(): pl.pallas_call(pack_kernel, in_specs=[HBM_SPEC] * 3, out_specs=[HBM_SPEC]...  5.62 us
  transfers between devices with their start and end apart: 3, of which 3 were waited for; matrix products, arithmetic and copies ran while one was open for 1% of the time, Pallas kernels for 25%

commit v1 on v0

--- a/solution.py
+++ b/solution.py
@@ -258,7 +258,6 @@
     grad_ref,
     terms_ref,
     probs_ref,
-    key_t_ref,
     out_ref,
     total_ref,
     held_ref,
@@ -303,8 +302,6 @@
                     total_ref[b] += terms[j * BLK : (j + 1) * BLK, :]
 
         by_count(live[tiles[0]], listed, body)
-        for slot in slots:
-            key_t_ref[slot] = key_ref[rows_of(step * GROUP + slot)].T
         return carry
 
     lax.fori_loop(0, GROUP // PROBS_TOGETHER, group_step, 0)
@@ -339,7 +336,6 @@
             in_specs=[whole(part, (0, place, 0)) for place in range(3)] + [HBM_SPEC],
             out_specs=[
                 pl.BlockSpec((GROUP, listed * BLK, BLK), lambda i, *_: (i, 0, 0)),
-                pl.BlockSpec((GROUP, DH, BLK), lambda i, *_: (i, 0, 0)),
                 whole((devices, rows + spare, DH)),
             ],
             scratch_shapes=[
@@ -350,7 +346,6 @@
         ),
         out_shape=[
             jax.ShapeDtypeStruct((tiles, listed * BLK, BLK), BF16),
-            jax.ShapeDtypeStruct((tiles, DH, BLK), BF16),
             pltpu.HBM((devices, rows + spare, DH), BF16),
         ],
         compiler_params=pltpu.CompilerParams(vmem_limit_bytes=KERNEL_LIMIT),
@@ -363,7 +358,7 @@
 
 
 def grads_kernel(
-    listed, pattern, live, order, query_ref, grad_ref, value_ref, key_t_ref, probs_ref, out_ref, total_ref
+    listed, pattern, live, order, query_ref, grad_ref, value_ref, key_ref, probs_ref, out_ref, total_ref, key_t_ref
 ):
     scale = DH ** (-0.5)
     step, steps = pl.program_id(0), pl.num_programs(0)
@@ -372,6 +367,14 @@
     @pl.when(step == 0)
     def _():
         clear(total_ref)
+
+        def transpose(group, carry):
+            for t in range(GROUP):
+                block = group * GROUP + t
+                key_t_ref[block] = key_ref[rows_of(block)].T
+            return carry
+
+        lax.fori_loop(0, key_t_ref.shape[0] // GROUP, transpose, 0)
 
     def group_step(group, carry):
         slots = [group * TOGETHER + t for t in range(TOGETHER)]
@@ -411,7 +414,7 @@
         lax.fori_loop(0, total_ref.shape[0], finish, 0)
 
 
-def grads_of(triple, rows, values, keys_t, probs, pattern, live_blocks, order):
+def grads_of(triple, rows, values, probs, pattern, live_blocks, order):
     tiles, listed = pattern.shape
     pairs = tiles * listed
     devices = triple.shape[0]
@@ -425,11 +428,14 @@
                 whole(part),
                 whole(part, (0, 2, 0)),
                 whole(part),
-                whole(keys_t.shape),
+                whole(part, (0, 1, 0)),
                 pl.BlockSpec((GROUP, listed * BLK, BLK), lambda i, *_: (i, 0, 0)),
             ],
             out_specs=whole((devices, 2 * rows, DH)),
-            scratch_shapes=[pltpu.VMEM((tiles, BLK, DH), F32)],
+            scratch_shapes=[
+                pltpu.VMEM((tiles, BLK, DH), F32),
+                pltpu.VMEM((tiles, DH, BLK), BF16),
+            ],
         ),
         out_shape=jax.ShapeDtypeStruct((devices, 2 * rows, DH), BF16),
         compiler_params=pltpu.CompilerParams(vmem_limit_bytes=KERNEL_LIMIT),
@@ -438,7 +444,7 @@
             bytes_accessed=2 * pairs * BLK * BLK + 16 * tiles * BLK * DH,
             transcendentals=0,
         ),
-    )(pattern.reshape(-1), live_blocks, order, triple, triple, values, keys_t, probs)
+    )(pattern.reshape(-1), live_blocks, order, triple, triple, values, triple, probs)
 
 
 def exchange(blocks):
@@ -464,11 +470,11 @@
     )
     values = exchange(values)
     order = order_by_count(live_blocks)
-    probs, keys_t, value_grad = probs_of(triple, rows, pattern, live_blocks, order, share)
+    probs, value_grad = probs_of(triple, rows, pattern, live_blocks, order, share)
 
     value_grad, values = lax.optimization_barrier((value_grad, values))
     value_grad = exchange(value_grad)
-    grads = grads_of(triple, rows, values, keys_t, probs, pattern, live_blocks, order)
+    grads = grads_of(triple, rows, values, probs, pattern, live_blocks, order)
     grads, value_grad = lax.optimization_barrier((grads, value_grad))
     grads = exchange(grads)
 

time: 254 us -> 254 us (level)
  transfers between devices with their start and end apart: 3 -> 3, of which waited for: 3 -> 3; matrix products, arithmetic and copies ran while one was open for 1% -> 1% of each run, Pallas kernels for 25% -> 24%
where the time goes in v1:
time: 254 us; the launch traced here: 253 us
  blocking collectives  151 us (59%)
  Pallas kernels  69.5 us (27%)
  waiting for transfers between devices  19 us (7%)
  starting transfers between devices  10.2 us (4%)
    all_to_all x2, blocking collectives, exchange(): lax.all_to_all(blocks, 'ctx', split_axis=0, concat_axis=0, tiled=True)  151 us
    pallas_call x1, Pallas kernels, grads_of(): pl.pallas_call(functools.partial(grads_kernel, listed), grid_spec=pltpu.P...  33.9 us
    pallas_call x1, Pallas kernels, probs_of(): pl.pallas_call(functools.partial(probs_kernel, listed), grid_spec=pltpu.P...  22.5 us
    all_to_all x2, waiting for transfers between devices, exchange(): lax.all_to_all(blocks, 'ctx', split_axis=0, concat_axis=0, tiled=True)  17.3 us
    all_to_all x2, starting transfers between devices, exchange(): lax.all_to_all(blocks, 'ctx', split_axis=0, concat_axis=0, tiled=True)  8.61 us
    pallas_call x1, Pallas kernels, pack(): pl.pallas_call(pack_kernel, in_specs=[HBM_SPEC] * 3, out_specs=[HBM_SPEC]...  5.62 us
  transfers between devices with their start and end apart: 3, of which 3 were waited for; matrix products, arithmetic and copies ran while one was open for 1% of the time, Pallas kernels for 24%

profile of v1, /device:TPU:0, one launch (start us, length us, event | category | flops | bytes accessed | tf_op | source)
XLA Modules:
  0.0 253.3 jit_solution(12529221370054386256)
XLA Ops:
  0.6 0.0 copy-start.2
  0.6 0.0 copy-start
  0.7 0.0 copy-start.1
  0.7 0.0 copy-start.3
  0.7 1.6 collective-permute-start
  2.2 5.6 %shard_map.120 = (bf16[32,880,128]{2,1,0:T(8,128)(2,1)}, bf16[32,256,128]{2,1,0:T(8,128)(2,1)}) custom-call(bf16[256,4096]{1,0:T(8,128)(2,1)} %query_ref.1, bf16[256,4096]{1,0:T(8,128)(2,1)} %key_ref.1, bf16[256,4096]{1,0:T(8,128)(2,1)} %value_ref.1), custom_call_target="tpu_custom_call" | custom-call | bytes 12582912 | tf_op jit(solution)/shard_map/pallas_call | solution.py:81
  7.9 1.7 collective-permute-done.next_ref
  9.5 0.0 copy-done.2
  9.5 0.0 copy-done
  9.5 0.0 copy-done.1
  9.5 0.0 copy-done.3
  9.5 3.5 %shard_map.121 = bf16[32,880,128]{2,1,0:T(8,128)(2,1)} custom-call(bf16[2,128,384]{2,1,0:T(8,128)(2,1)S(1)} %copy-done.2, bf16[2,128,384]{2,1,0:T(8,128)(2,1)S(1)} %collective-permute-done.next_ref, bf16[2,128,384]{2,1,0:T(8,128)(2,1)S(1)} %copy-done.3, bf16[3,384,384]{2,1,0:T(8,128)(2,1)S(1)} %copy-done.1, ...), custom_call_target="tpu_custom_call", output_to_operand_aliasing={{}: (5, {})} | custom-call | flops 805306368 | bytes 6291456 | tf_op jit(solution)/shard_map/pallas_call | solution.py:166
  13.0 95.9 %all_to_all.20.query_ref.key_ref.grad_ref.terms_ref = bf16[32,880,128]{2,1,0:T(8,128)(2,1)} all-to-all(bf16[32,880,128]{2,1,0:T(8,128)(2,1)} %shard_map.121), channel_id=1, replica_groups=mesh['clip'=4,'ctx'=32] {'ctx'}, dimensions={0} | all-to-all | bytes 14417920 | tf_op jit(solution)/shard_map/all_to_all | solution.py:451
  108.9 0.0 copy-start.5
  108.9 0.0 copy-start.6
  108.9 4.3 %all-to-all-start.1 = ((bf16[32,256,128]{2,1,0:T(8,128)(2,1)}), bf16[32,256,128]{2,1,0:T(8,128)(2,1)S(1)}, u32[]{:S(2)}, u32[]{:S(2)}) async-start(bf16[32,256,128]{2,1,0:T(8,128)(2,1)} %get-tuple-element.28), calls=%async_computation.1 | async-start | bytes 4194304 | tf_op jit(solution)/shard_map/all_to_all | solution.py:451
  113.2 0.0 copy-done.5
  113.2 0.1 copy.15
  113.3 0.7 reshape.15.pattern
  114.0 0.0 copy-done.6
  114.0 0.2 convert_reduce_fusion
  114.2 0.6 select_reduce_fusion.order
  114.8 22.5 %shard_map.122 = (bf16[64,1024,128]{2,1,0:T(8,128)(2,1)}, bf16[32,368,128]{2,1,0:T(8,128)(2,1)}) custom-call(s32[512]{0:T(512)} %reshape.15.pattern, s32[64]{0:T(128)} %live.1, s32[64]{0:T(128)} %select_reduce_fusion.order, bf16[32,880,128]{2,1,0:T(8,128)(2,1)} %all_to_all.20.query_ref.key_ref.grad_ref.terms_ref, ...), custom_call_target="tpu_custom_call" | custom-call | flops 4294967296 | bytes 16777216 | tf_op jit(solution)/shard_map/pallas_call | solution.py:331
  137.3 7.8 %all-to-all-done.1.value_ref = bf16[32,256,128]{2,1,0:T(8,128)(2,1)S(1)} async-done(((bf16[32,256,128]{2,1,0:T(8,128)(2,1)}), bf16[32,256,128]{2,1,0:T(8,128)(2,1)S(1)}, u32[]{:S(2)}, u32[]{:S(2)}) %all-to-all-start.1) | async-done | bytes 2097184 | tf_op jit(solution)/shard_map/all_to_all | solution.py:451
  145.1 0.0 copy-start.4
  145.1 1.3 copy-done.4
  146.4 4.3 %all-to-all-start.2 = ((bf16[32,368,128]{2,1,0:T(8,128)(2,1)}), bf16[32,368,128]{2,1,0:T(8,128)(2,1)S(1)}, u32[]{:S(2)}, u32[]{:S(2)}) async-start(bf16[32,368,128]{2,1,0:T(8,128)(2,1)} %get-tuple-element.31), calls=%async_computation.2 | async-start | bytes 6029312 | tf_op jit(solution)/shard_map/all_to_all | solution.py:451
  150.7 33.9 %shard_map.123 = bf16[32,512,128]{2,1,0:T(8,128)(2,1)} custom-call(s32[512]{0:T(512)} %reshape.15.pattern, s32[64]{0:T(128)} %live.1, s32[64]{0:T(128)} %select_reduce_fusion.order, bf16[32,880,128]{2,1,0:T(8,128)(2,1)} %all_to_all.20.query_ref.key_ref.grad_ref.terms_ref, bf16[32,880,128]{2,1,0:T(8,128)(2,1)} %all_to_all.20.query_ref.key_ref.grad_ref.terms_ref, ...), custom_call_target="tpu_custom_call" | custom-call | flops 6442450944 | bytes 33554432 | tf_op jit(solution)/shard_map/pallas_call | solution.py:422
  184.6 9.5 %all-to-all-done.2.last_ref = bf16[32,368,128]{2,1,0:T(8,128)(2,1)S(1)} async-done(((bf16[32,368,128]{2,1,0:T(8,128)(2,1)}), bf16[32,368,128]{2,1,0:T(8,128)(2,1)S(1)}, u32[]{:S(2)}, u32[]{:S(2)}) %all-to-all-start.2) | async-done | bytes 3014688 | tf_op jit(solution)/shard_map/all_to_all | solution.py:451
  194.1 55.0 %all_to_all.21.pair_ref = bf16[32,512,128]{2,1,0:T(8,128)(2,1)S(1)} all-to-all(bf16[32,512,128]{2,1,0:T(8,128)(2,1)} %shard_map.123), channel_id=1, replica_groups=mesh['clip'=4,'ctx'=32] {'ctx'}, dimensions={0} | all-to-all | bytes 8388608 | tf_op jit(solution)/shard_map/all_to_all | solution.py:451
  249.1 4.0 %shard_map.124 = (bf16[256,4096]{1,0:T(8,128)(2,1)}, bf16[256,4096]{1,0:T(8,128)(2,1)}, bf16[256,4096]{1,0:T(8,128)(2,1)}, f32[3,384,384]{2,1,0:T(8,128)}) custom-call(bf16[32,512,128]{2,1,0:T(8,128)(2,1)S(1)} %all_to_all.21.pair_ref, bf16[32,368,128]{2,1,0:T(8,128)(2,1)S(1)} %all-to-all-done.2.last_ref), custom_call_target="tpu_custom_call" | custom-call | bytes 12582912 | tf_op jit(solution)/shard_map/pallas_call | solution.py:218
Async XLA Ops:
  0.6 8.9 %copy-start.2 = (bf16[2,128,384]{2,1,0:T(8,128)(2,1)S(1)}, bf16[2,128,384]{2,1,0:T(8,128)(2,1)}, u32[]{:S(2)}) copy-start(bf16[2,128,384]{2,1,0:T(8,128)(2,1)} %near_ref.1) | copy-start | bytes 589828
  0.6 8.9 %copy-start = (bf16[4096,384]{1,0:T(8,128)(2,1)S(1)}, bf16[4096,384]{1,0:T(8,128)(2,1)}, u32[]{:S(2)}) copy-start(bf16[4096,384]{1,0:T(8,128)(2,1)} %head_weight_ref.1) | copy-start | bytes 9437188
  0.7 8.9 %copy-start.1 = (bf16[3,384,384]{2,1,0:T(8,128)(2,1)S(1)}, bf16[3,384,384]{2,1,0:T(8,128)(2,1)}, u32[]{:S(2)}) copy-start(bf16[3,384,384]{2,1,0:T(8,128)(2,1)} %tap_weight_ref.1) | copy-start | bytes 2654212
  0.7 8.9 %copy-start.3 = (bf16[2,128,384]{2,1,0:T(8,128)(2,1)S(1)}, bf16[2,128,384]{2,1,0:T(8,128)(2,1)}, u32[]{:S(2)}) copy-start(bf16[2,128,384]{2,1,0:T(8,128)(2,1)} %feature_ref.1) | copy-start | bytes 589828
  0.7 8.8 %collective-permute-start = (bf16[2,128,384]{2,1,0:T(8,128)(2,1)}, bf16[2,128,384]{2,1,0:T(8,128)(2,1)S(1)}, u32[]{:S(2)}, u32[]{:S(2)}) collective-permute-start(bf16[2,128,384]{2,1,0:T(8,128)(2,1)} %near_ref.1), channel_id=1, source_target_pairs={{1,0},{2,1},{3,2},{4,3},{5,4},{6,5},{7,6},{8,7},{9,8},{10,9},{11,1... | collective-permute-start | bytes 589832 | tf_op jit(solution)/shard_map/ppermute | solution.py:462
  108.9 4.3 %copy-start.5 = (s32[64,8]{0,1:T(8,128)S(1)}, s32[64,8]{0,1:T(8,128)}, u32[]{:S(2)}) copy-start(s32[64,8]{0,1:T(8,128)} %param.16) | copy-start | bytes 6148
  108.9 5.1 %copy-start.6 = (s32[64]{0:T(128)S(1)}, s32[64]{0:T(128)}, u32[]{:S(2)}) copy-start(s32[64]{0:T(128)} %live.1) | copy-start | bytes 772
  108.9 36.2 %all-to-all-start.1 = ((bf16[32,256,128]{2,1,0:T(8,128)(2,1)}), bf16[32,256,128]{2,1,0:T(8,128)(2,1)S(1)}, u32[]{:S(2)}, u32[]{:S(2)}) async-start(bf16[32,256,128]{2,1,0:T(8,128)(2,1)} %get-tuple-element.28), calls=%async_computation.1 | async-start | bytes 4194304 | tf_op jit(solution)/shard_map/all_to_all | solution.py:451
  145.1 1.3 copy-start.4
  146.4 47.7 %all-to-all-start.2 = ((bf16[32,368,128]{2,1,0:T(8,128)(2,1)}), bf16[32,368,128]{2,1,0:T(8,128)(2,1)S(1)}, u32[]{:S(2)}, u32[]{:S(2)}) async-start(bf16[32,368,128]{2,1,0:T(8,128)(2,1)} %get-tuple-element.31), calls=%async_computation.2 | async-start | bytes 6029312 | tf_op jit(solution)/shard_map/all_to_all | solution.py:451

commit v2 on v1

--- a/solution.py
+++ b/solution.py
@@ -461,15 +461,13 @@
 
     incoming = lax.ppermute(feat_grad, "ctx", [(i + 1, i) for i in range(devices - 1)])
     triple, values = pack(queries, keys, values, share)
-    triple, values, incoming = lax.optimization_barrier((triple, values, incoming))
+    order = order_by_count(live_blocks)
+    triple, values, incoming, order = lax.optimization_barrier((triple, values, incoming, order))
     triple = decoder(feat_grad, incoming, features, conv_weight, head_weight, triple)
 
     triple = exchange(triple)
-    values, triple, pattern, live_blocks = lax.optimization_barrier(
-        (values, triple, pattern, live_blocks)
-    )
+    values, triple = lax.optimization_barrier((values, triple))
     values = exchange(values)
-    order = order_by_count(live_blocks)
     probs, value_grad = probs_of(triple, rows, pattern, live_blocks, order, share)
 
     value_grad, values = lax.optimization_barrier((value_grad, values))

time: 254 us -> 253 us (level)
  blocking collectives: 151 us -> 148 us
where the time goes in v2:
time: 253 us; the launch traced here: 251 us
  blocking collectives  148 us (58%)
  Pallas kernels  68.3 us (27%)
  waiting for transfers between devices  19.9 us (8%)
  starting transfers between devices  10.2 us (4%)
    all_to_all x2, blocking collectives, exchange(): lax.all_to_all(blocks, 'ctx', split_axis=0, concat_axis=0, tiled=True)  148 us
    pallas_call x1, Pallas kernels, grads_of(): pl.pallas_call(functools.partial(grads_kernel, listed), grid_spec=pltpu.P...  32.6 us
    pallas_call x1, Pallas kernels, probs_of(): pl.pallas_call(functools.partial(probs_kernel, listed), grid_spec=pltpu.P...  22.5 us
    all_to_all x2, waiting for transfers between devices, exchange(): lax.all_to_all(blocks, 'ctx', split_axis=0, concat_axis=0, tiled=True)  19.1 us
    all_to_all x2, starting transfers between devices, exchange(): lax.all_to_all(blocks, 'ctx', split_axis=0, concat_axis=0, tiled=True)  8.61 us
    pallas_call x1, Pallas kernels, pack(): pl.pallas_call(pack_kernel, in_specs=[HBM_SPEC] * 3, out_specs=[HBM_SPEC]...  5.62 us
  transfers between devices with their start and end apart: 3, of which 3 were waited for; matrix products, arithmetic and copies ran while one was open for 1% of the time, Pallas kernels for 24%

profile of v2, /device:TPU:0, one launch (start us, length us, event | category | flops | bytes accessed | tf_op | source)
XLA Modules:
  0.0 250.7 jit_solution(2043250582332400070)
XLA Ops:
  0.6 0.0 copy-start.2
  0.6 0.0 copy-start.6
  0.7 0.0 copy-start
  0.7 0.0 copy-start.1
  0.7 0.0 copy-start.3
  0.7 1.6 collective-permute-start
  2.2 5.6 %shard_map.120 = (bf16[32,880,128]{2,1,0:T(8,128)(2,1)}, bf16[32,256,128]{2,1,0:T(8,128)(2,1)}) custom-call(bf16[256,4096]{1,0:T(8,128)(2,1)} %query_ref.1, bf16[256,4096]{1,0:T(8,128)(2,1)} %key_ref.1, bf16[256,4096]{1,0:T(8,128)(2,1)} %value_ref.1), custom_call_target="tpu_custom_call" | custom-call | bytes 12582912 | tf_op jit(solution)/shard_map/pallas_call | solution.py:81
  7.9 0.0 copy-done.6
  7.9 0.2 convert_reduce_fusion
  8.1 0.6 select_reduce_fusion.order
  8.7 0.8 collective-permute-done.next_ref
  9.5 0.0 copy-done.2
  9.5 0.0 copy-done
  9.5 0.0 copy-done.1
  9.5 0.0 copy-done.3
  9.6 3.5 %shard_map.121 = bf16[32,880,128]{2,1,0:T(8,128)(2,1)} custom-call(bf16[2,128,384]{2,1,0:T(8,128)(2,1)S(1)} %copy-done.2, bf16[2,128,384]{2,1,0:T(8,128)(2,1)S(1)} %collective-permute-done.next_ref, bf16[2,128,384]{2,1,0:T(8,128)(2,1)S(1)} %copy-done.3, bf16[3,384,384]{2,1,0:T(8,128)(2,1)S(1)} %copy-done.1, ...), custom_call_target="tpu_custom_call", output_to_operand_aliasing={{}: (5, {})} | custom-call | flops 805306368 | bytes 6291456 | tf_op jit(solution)/shard_map/pallas_call | solution.py:166
  13.0 95.9 %all_to_all.20.query_ref.key_ref.grad_ref.terms_ref = bf16[32,880,128]{2,1,0:T(8,128)(2,1)} all-to-all(bf16[32,880,128]{2,1,0:T(8,128)(2,1)} %shard_map.121), channel_id=1, replica_groups=mesh['clip'=4,'ctx'=32] {'ctx'}, dimensions={0} | all-to-all | bytes 14417920 | tf_op jit(solution)/shard_map/all_to_all | solution.py:451
  108.9 0.0 copy-start.5
  108.9 4.3 %all-to-all-start.1 = ((bf16[32,256,128]{2,1,0:T(8,128)(2,1)}), bf16[32,256,128]{2,1,0:T(8,128)(2,1)S(1)}, u32[]{:S(2)}, u32[]{:S(2)}) async-start(bf16[32,256,128]{2,1,0:T(8,128)(2,1)} %get-tuple-element.26), calls=%async_computation.1 | async-start | bytes 4194304 | tf_op jit(solution)/shard_map/all_to_all | solution.py:451
  113.2 0.0 copy-done.5
  113.3 0.1 copy.15
  113.3 0.7 reshape.15.pattern
  114.0 22.5 %shard_map.122 = (bf16[64,1024,128]{2,1,0:T(8,128)(2,1)}, bf16[32,368,128]{2,1,0:T(8,128)(2,1)}) custom-call(s32[512]{0:T(512)} %reshape.15.pattern, s32[64]{0:T(128)} %live.3, s32[64]{0:T(128)} %select_reduce_fusion.order, bf16[32,880,128]{2,1,0:T(8,128)(2,1)} %all_to_all.20.query_ref.key_ref.grad_ref.terms_ref, ...), custom_call_target="tpu_custom_call" | custom-call | flops 4294967296 | bytes 16777216 | tf_op jit(solution)/shard_map/pallas_call | solution.py:331
  136.5 7.6 %all-to-all-done.1.value_ref = bf16[32,256,128]{2,1,0:T(8,128)(2,1)S(1)} async-done(((bf16[32,256,128]{2,1,0:T(8,128)(2,1)}), bf16[32,256,128]{2,1,0:T(8,128)(2,1)S(1)}, u32[]{:S(2)}, u32[]{:S(2)}) %all-to-all-start.1) | async-done | bytes 2097184 | tf_op jit(solution)/shard_map/all_to_all | solution.py:451
  144.1 0.0 copy-start.4
  144.1 1.3 copy-done.4
  145.4 4.3 %all-to-all-start.2 = ((bf16[32,368,128]{2,1,0:T(8,128)(2,1)}), bf16[32,368,128]{2,1,0:T(8,128)(2,1)S(1)}, u32[]{:S(2)}, u32[]{:S(2)}) async-start(bf16[32,368,128]{2,1,0:T(8,128)(2,1)} %get-tuple-element.29), calls=%async_computation.2 | async-start | bytes 6029312 | tf_op jit(solution)/shard_map/all_to_all | solution.py:451
  149.7 32.6 %shard_map.123 = bf16[32,512,128]{2,1,0:T(8,128)(2,1)} custom-call(s32[512]{0:T(512)} %reshape.15.pattern, s32[64]{0:T(128)} %live.3, s32[64]{0:T(128)} %select_reduce_fusion.order, bf16[32,880,128]{2,1,0:T(8,128)(2,1)} %all_to_all.20.query_ref.key_ref.grad_ref.terms_ref, bf16[32,880,128]{2,1,0:T(8,128)(2,1)} %all_to_all.20.query_ref.key_ref.grad_ref.terms_ref, ...), custom_call_target="tpu_custom_call" | custom-call | flops 6442450944 | bytes 33554432 | tf_op jit(solution)/shard_map/pallas_call | solution.py:422
  182.3 11.5 %all-to-all-done.2.last_ref = bf16[32,368,128]{2,1,0:T(8,128)(2,1)S(1)} async-done(((bf16[32,368,128]{2,1,0:T(8,128)(2,1)}), bf16[32,368,128]{2,1,0:T(8,128)(2,1)S(1)}, u32[]{:S(2)}, u32[]{:S(2)}) %all-to-all-start.2) | async-done | bytes 3014688 | tf_op jit(solution)/shard_map/all_to_all | solution.py:451
  193.9 52.6 %all_to_all.21.pair_ref = bf16[32,512,128]{2,1,0:T(8,128)(2,1)S(1)} all-to-all(bf16[32,512,128]{2,1,0:T(8,128)(2,1)} %shard_map.123), channel_id=1, replica_groups=mesh['clip'=4,'ctx'=32] {'ctx'}, dimensions={0} | all-to-all | bytes 8388608 | tf_op jit(solution)/shard_map/all_to_all | solution.py:451
  246.5 4.0 %shard_map.124 = (bf16[256,4096]{1,0:T(8,128)(2,1)}, bf16[256,4096]{1,0:T(8,128)(2,1)}, bf16[256,4096]{1,0:T(8,128)(2,1)}, f32[3,384,384]{2,1,0:T(8,128)}) custom-call(bf16[32,512,128]{2,1,0:T(8,128)(2,1)S(1)} %all_to_all.21.pair_ref, bf16[32,368,128]{2,1,0:T(8,128)(2,1)S(1)} %all-to-all-done.2.last_ref), custom_call_target="tpu_custom_call" | custom-call | bytes 12582912 | tf_op jit(solution)/shard_map/pallas_call | solution.py:218
Async XLA Ops:
  0.6 8.9 %copy-start.2 = (bf16[2,128,384]{2,1,0:T(8,128)(2,1)S(1)}, bf16[2,128,384]{2,1,0:T(8,128)(2,1)}, u32[]{:S(2)}) copy-start(bf16[2,128,384]{2,1,0:T(8,128)(2,1)} %near_ref.1) | copy-start | bytes 589828
  0.6 7.2 %copy-start.6 = (s32[64]{0:T(128)S(1)}, s32[64]{0:T(128)}, u32[]{:S(2)}) copy-start(s32[64]{0:T(128)} %live.3) | copy-start | bytes 772
  0.7 8.9 %copy-start = (bf16[4096,384]{1,0:T(8,128)(2,1)S(1)}, bf16[4096,384]{1,0:T(8,128)(2,1)}, u32[]{:S(2)}) copy-start(bf16[4096,384]{1,0:T(8,128)(2,1)} %head_weight_ref.1) | copy-start | bytes 9437188
  0.7 8.9 %copy-start.1 = (bf16[3,384,384]{2,1,0:T(8,128)(2,1)S(1)}, bf16[3,384,384]{2,1,0:T(8,128)(2,1)}, u32[]{:S(2)}) copy-start(bf16[3,384,384]{2,1,0:T(8,128)(2,1)} %tap_weight_ref.1) | copy-start | bytes 2654212
  0.7 8.9 %copy-start.3 = (bf16[2,128,384]{2,1,0:T(8,128)(2,1)S(1)}, bf16[2,128,384]{2,1,0:T(8,128)(2,1)}, u32[]{:S(2)}) copy-start(bf16[2,128,384]{2,1,0:T(8,128)(2,1)} %feature_ref.1) | copy-start | bytes 589828
  0.7 8.8 %collective-permute-start = (bf16[2,128,384]{2,1,0:T(8,128)(2,1)}, bf16[2,128,384]{2,1,0:T(8,128)(2,1)S(1)}, u32[]{:S(2)}, u32[]{:S(2)}) collective-permute-start(bf16[2,128,384]{2,1,0:T(8,128)(2,1)} %near_ref.1), channel_id=1, source_target_pairs={{1,0},{2,1},{3,2},{4,3},{5,4},{6,5},{7,6},{8,7},{9,8},{10,9},{11,1... | collective-permute-start | bytes 589832 | tf_op jit(solution)/shard_map/ppermute | solution.py:462
  108.9 4.3 %copy-start.5 = (s32[64,8]{0,1:T(8,128)S(1)}, s32[64,8]{0,1:T(8,128)}, u32[]{:S(2)}) copy-start(s32[64,8]{0,1:T(8,128)} %param.16) | copy-start | bytes 6148
  108.9 35.2 %all-to-all-start.1 = ((bf16[32,256,128]{2,1,0:T(8,128)(2,1)}), bf16[32,256,128]{2,1,0:T(8,128)(2,1)S(1)}, u32[]{:S(2)}, u32[]{:S(2)}) async-start(bf16[32,256,128]{2,1,0:T(8,128)(2,1)} %get-tuple-element.26), calls=%async_computation.1 | async-start | bytes 4194304 | tf_op jit(solution)/shard_map/all_to_all | solution.py:451
  144.1 1.3 copy-start.4
  145.4 48.4 %all-to-all-start.2 = ((bf16[32,368,128]{2,1,0:T(8,128)(2,1)}), bf16[32,368,128]{2,1,0:T(8,128)(2,1)S(1)}, u32[]{:S(2)}, u32[]{:S(2)}) async-start(bf16[32,368,128]{2,1,0:T(8,128)(2,1)} %get-tuple-element.29), calls=%async_computation.2 | async-start | bytes 6029312 | tf_op jit(solution)/shard_map/all_to_all | solution.py:451
